TPU v7x, 1024 devices: a whole 4x8x16 slice. The times are simulated.
1024 devices in a mesh: dp: 128 (over z, y), grp: 8 (over x, core).
Axes of the slice: x: 4, y: 8, z: 16, core: 2. Of those that a mesh axis runs over, the one named last changes fastest.
Arguments:
- user_vec: bfloat16 [32768, 256], P('dp'), may hold values from -40 to 40
- item_emb: bfloat16 [32768, 256], P(('dp', 'grp')), may hold values from -40 to 40
- w_one: bfloat16 [256, 1024], replicated, may hold values from -0.375 to 0.375
- w_two: bfloat16 [1024, 256], replicated, may hold values from -0.1875 to 0.1875
- item_owner: int32 [32768, 2], P(('dp', 'grp')), may hold values from 0 to 7, all different within a row; in each aligned block of 32 rows (0 to 31, 32 to 63, ...) at most 16 rows name the same one
- item_slot: int32 [32768, 2], P(('dp', 'grp')), may hold values from 0 to 63
Outputs:
- table_grad: float32 [65536, 256], P(('dp', 'grp'))
- w_grads: float32 [1024, 512], P(('dp', 'grp'))
Inputs may be any that keep to these rules, and one draw needn't show every extreme that they name: `item_owner`: the two owners of an item differ. Among the rows of one device each owner index is named by at most 16 rows, and by exactly 16 on some devices.
All inputs are finite; a program needn't handle non-finite values.
Results may differ from a plain program's by a relative error of at most 0.015.
Values may be sent and summed in bfloat16 or wider, within the bound.
No kernel may reach another device: no remote copies, remote signals or barrier semaphores. Data moves between devices by JAX's collectives and lax.ppermute only.
A program may use at most 32 MiB of HBM per device.

v0:
```python
import jax
import jax.numpy as jnp
from jax import lax
from jax.sharding import PartitionSpec as P

TOUCH = 64


sharpness_divisor = 0.02
epsilon = 1e-06


def unit_rows(values):
    return values * lax.rsqrt(jnp.sum(values * values, axis=-1, keepdims=True) + epsilon)


def silu_slope(preact):
    sigmoid = jax.nn.sigmoid(preact)
    return (preact * sigmoid, sigmoid * (1.0 + preact * (1.0 - sigmoid)))


def contract_first(left, right):
    return lax.dot_general(
        left, right, (((0,), (0,)), ((), ())), preferred_element_type=jnp.float32
    )


def reduce_trailing_dimension(left, right):
    return lax.dot_general(
        left, right, (((1,), (1,)), ((), ())), preferred_element_type=jnp.float32
    )


def on_device(user_vec, item_emb, w_one, w_two, item_owner, item_slot):
    groups = lax.axis_size("grp")
    dp_count = lax.axis_size("dp")
    grp_index = lax.axis_index("grp")
    dp_index = lax.axis_index("dp")
    per_dev = item_emb.shape[0]
    emb_width = item_emb.shape[1]
    out_width = w_two.shape[1]
    hidden_width = w_one.shape[1]
    user_rows = user_vec.shape[0]
    query_unit_vectors = unit_rows(user_vec.astype(jnp.float32)).astype(jnp.bfloat16)
    preact = jnp.dot(item_emb, w_one, preferred_element_type=jnp.float32)
    hidden_f, slopes = silu_slope(preact)
    hidden = hidden_f.astype(jnp.bfloat16)
    item_out = jnp.dot(hidden, w_two, preferred_element_type=jnp.float32)
    item_scale = lax.rsqrt(jnp.sum(item_out * item_out, axis=1, keepdims=True) + epsilon)
    item_dir = item_out * item_scale
    candidate_unit_vectors = item_dir.astype(jnp.bfloat16)
    distractor_candidates = lax.all_gather(candidate_unit_vectors, "dp", axis=0, tiled=True)
    angle_similarity_scores = (
        reduce_trailing_dimension(query_unit_vectors, distractor_candidates) / sharpness_divisor
    )
    powers = jnp.exp(angle_similarity_scores)
    totals = lax.psum(jnp.sum(powers, axis=1), "grp")
    row_ids = jnp.arange(user_rows, dtype=jnp.int32)
    columns = jnp.arange(distractor_candidates.shape[0], dtype=jnp.int32)
    positive_col = dp_index * per_dev + row_ids % per_dev
    is_positive = (row_ids // per_dev == grp_index)[:, None] & (
        columns[None, :] == positive_col[:, None]
    )
    logit_cot = (powers / totals[:, None] - is_positive.astype(jnp.float32)).astype(jnp.bfloat16)
    unit_cot = lax.psum_scatter(
        contract_first(logit_cot, query_unit_vectors), "dp", scatter_dimension=0, tiled=True
    )
    along = jnp.sum(item_dir * unit_cot, axis=1, keepdims=True)
    out_cot = ((unit_cot - item_dir * along) * item_scale).astype(jnp.bfloat16)
    preact_cot = (reduce_trailing_dimension(out_cot, w_two) * slopes).astype(jnp.bfloat16)
    emb_cot = reduce_trailing_dimension(preact_cot, w_one)
    factors = jnp.concatenate([item_emb, out_cot], axis=1)
    group_rows = lax.all_gather(factors, "grp", axis=0, tiled=True)
    emb_all = group_rows[:, :emb_width]
    cot_all = group_rows[:, emb_width:]
    per_rank = hidden_width // (dp_count * groups)
    w_one_sel = lax.dynamic_index_in_dim(
        w_one.reshape(emb_width, dp_count, groups, per_rank), grp_index, axis=2, keepdims=False
    )
    w_one_sel = w_one_sel.reshape(emb_width, dp_count * per_rank)
    w_two_sel = lax.dynamic_index_in_dim(
        w_two.reshape(dp_count, groups, per_rank, out_width), grp_index, axis=1, keepdims=False
    )
    w_two_sel = w_two_sel.reshape(dp_count * per_rank, out_width)
    preact_sel = jnp.dot(emb_all, w_one_sel, preferred_element_type=jnp.float32)
    hidden_sel, slopes_sel = silu_slope(preact_sel)
    preact_cot_sel = (reduce_trailing_dimension(cot_all, w_two_sel) * slopes_sel).astype(
        jnp.bfloat16
    )
    partials = jnp.concatenate(
        [
            contract_first(preact_cot_sel, emb_all),
            contract_first(hidden_sel.astype(jnp.bfloat16), cot_all),
        ],
        axis=1,
    )
    w_grads = lax.psum_scatter(partials, "dp", scatter_dimension=0, tiled=True)
    entries = jnp.stack([emb_cot, emb_cot], axis=1).reshape(2 * per_dev, emb_width)
    owner_flat = item_owner.reshape(-1)
    slot_flat = item_slot.reshape(-1)
    target = owner_flat * TOUCH + slot_flat
    placing = (target[None, :] == jnp.arange(groups * TOUCH, dtype=jnp.int32)[:, None]).astype(
        jnp.float32
    )
    dense_rows = jnp.dot(placing, entries, precision=lax.Precision.HIGHEST)
    table_grad = lax.psum_scatter(
        dense_rows.astype(jnp.bfloat16), "grp", scatter_dimension=0, tiled=True
    ).astype(jnp.float32)
    return (table_grad, w_grads)


def solution(mesh):
    placed = (
        P("dp", None),
        P(("dp", "grp"), None),
        P(),
        P(),
        P(("dp", "grp"), None),
        P(("dp", "grp"), None),
    )
    return jax.shard_map(
        on_device,
        mesh=mesh,
        in_specs=placed,
        out_specs=(P(("dp", "grp"), None), P(("dp", "grp"), None)),
        check_vma=False,
    )
```

profile of v0, /device:TPU:1, one launch (start us, length us, event | category | flops | bytes accessed | tf_op | source)
XLA Modules:
  0.0 1287.9 jit_solution(18377782803205257328)
XLA Ops:
  7.2 0.0 copy-start
  7.2 0.0 copy-start.2
  7.2 0.0 all-gather.2.cloned.1.call-start
  7.2 1.3 fusion.48
  8.5 0.0 copy-done
  8.6 0.3 multiply_reduce_fusion.1
  8.9 0.7 multiply_convert_fusion.5
  9.6 0.0 all-gather.2.cloned.1.call-update
  9.6 0.0 reduce-scatter.3.cloned.1.call-start
  9.7 1.0 fusion.9
  10.7 149.0 %all-gather.2.cloned.1.call-done = bf16[4096,256]{1,0:T(8,128)(2,1)} async-done(((bf16[32,256]{1,0:T(8,128)(2,1)}), bf16[4096,256]{1,0:T(8,128)(2,1)}) %all-gather.2.cloned.1.call-update) | async-done | bytes 2097168 | tf_op jit(solution)/shard_map/all_gather | solution.py:52
  159.7 4.4 fusion.47
  164.0 21.4 %psum.7 = f32[256]{0:T(256)S(1)} all-reduce(f32[256]{0:T(256)S(1)} %get-tuple-element.4), channel_id=1, replica_groups=mesh['dp'=128,'grp'=8] {'grp'}, use_global_device_ids=true, to_apply=%region_3.0 | all-reduce | flops 256 | bytes 2048 | tf_op jit(solution)/shard_map/psum | solution.py:57
  185.5 0.0 copy-done.2
  185.5 5.7 fusion.2
  191.2 0.0 copy-start.1
  191.2 0.0 copy-start.4
  191.2 0.0 copy-start.5
  191.2 0.0 copy-start.3
  191.2 0.0 reduce-scatter.3.cloned.1.call-update
  191.2 0.0 all-reduce.3.cloned.1.call-start
  191.3 1.0 copy-done.1
  192.3 0.2 copy.19
  192.5 0.1 constant_dynamic-slice_fusion.1
  192.6 0.1 copy.20
  192.7 0.0 copy-done.4
  192.8 0.0 copy-done.5
  192.8 0.1 copy.17
  192.9 0.1 add.84
  193.0 0.1 constant_dynamic-slice_fusion.2
  193.1 753.3 %reduce-scatter.3.cloned.1.call-done = f32[32,256]{1,0:T(8,128)} async-done(((f32[4096,256]{1,0:T(8,128)}), f32[32,256]{1,0:T(8,128)}) %reduce-scatter.3.cloned.1.call-update) | async-done | bytes 32784 | tf_op jit(solution)/shard_map/reduce_scatter | solution.py:65
  946.5 0.9 multiply_reduce_fusion
  947.4 0.8 multiply_convert_fusion.4
  948.2 0.0 copy-done.3
  948.3 0.5 fusion.8
  948.8 24.5 %all_gather.7 = bf16[256,512]{1,0:T(8,128)(2,1)S(1)} all-gather(bf16[32,512]{1,0:T(8,128)(2,1)S(1)} %pad_maximum_fusion.2), channel_id=1, replica_groups=mesh['dp'=128,'grp'=8] {'grp'}, dimensions={0}, use_global_device_ids=true | all-gather | bytes 294912 | tf_op jit(solution)/shard_map/all_gather | solution.py:73
  973.2 0.2 fusion.21
  973.4 0.2 fusion.23
  973.6 0.4 fusion.7
  974.1 0.7 pad_maximum_fusion
  974.8 0.0 all-reduce.3.cloned.1.call-update
  974.8 0.0 reduce-scatter.5.cloned.1.call-start
  974.9 0.1 copy.18
  975.0 1.1 convolution_convert_fusion
  976.1 0.0 reduce-scatter.5.cloned.1.call-update
  976.1 1.3 dynamic-slice
  977.4 254.1 %all-reduce.3.cloned.1.call-done = f32[128,512]{1,0:T(8,128)} async-done(((f32[128,512]{1,0:T(8,128)}), f32[128,512]{1,0:T(8,128)}) %all-reduce.3.cloned.1.call-update) | async-done | bytes 262160
  1231.5 1.9 constant_dynamic-slice_fusion
  1233.4 46.5 %reduce-scatter.5.cloned.1.call-done = bf16[64,256]{1,0:T(8,128)(2,1)} async-done(((bf16[512,256]{1,0:T(8,128)(2,1)}), bf16[64,256]{1,0:T(8,128)(2,1)}) %reduce-scatter.5.cloned.1.call-update) | async-done | bytes 32784 | tf_op jit(solution)/shard_map/reduce_scatter | solution.py:106
  1279.9 1.4 convert_element_type.46
  (8 shorter events, 0.1 us)
Async XLA Ops:
  7.2 1.4 copy-start
  7.2 178.3 %copy-start.2 = (bf16[256,256]{1,0:T(8,128)(2,1)S(1)}, bf16[256,256]{1,0:T(8,128)(2,1)}, u32[]{:S(2)}) copy-start(bf16[256,256]{1,0:T(8,128)(2,1)} %param.6) | copy-start | bytes 393220
  7.2 152.5 %all-gather.2.cloned.1.call-start = ((), (), s32[]{:S(2)}) async-start(), calls=%async_computation.2 | async-start | bytes 2113536 | tf_op jit(solution)/shard_map/all_gather | solution.py:52
  9.6 936.9 %reduce-scatter.3.cloned.1.call-start = ((), (), s32[]{:S(2)}) async-start(), calls=%async_computation.3 | async-start | bytes 4227072 | tf_op jit(solution)/shard_map/reduce_scatter | solution.py:65
  191.2 1.0 copy-start.1
  191.2 1.5 copy-start.4
  191.2 1.5 copy-start.5
  191.2 757.0 %copy-start.3 = (bf16[32,256]{1,0:T(8,128)(2,1)S(1)}, bf16[32,256]{1,0:T(8,128)(2,1)}, u32[]{:S(2)}) copy-start(bf16[32,256]{1,0:T(8,128)(2,1)} %param.7) | copy-start | bytes 49156
  191.2 1040.2 %all-reduce.3.cloned.1.call-start = ((), (), s32[]{:S(2)}) async-start(), calls=%async_computation.5 | async-start | bytes 524288
  974.8 305.1 %reduce-scatter.5.cloned.1.call-start = ((), (), s32[]{:S(2)}) async-start(), calls=%async_computation.4 | async-start | bytes 294912 | tf_op jit(solution)/shard_map/reduce_scatter | solution.py:106
Sparse Core Ops, SparseCore 0:
  12.7 146.9 all-gather.1
  191.4 755.0 reduce-scatter.2
  974.9 256.4 all-reduce.2
  1234.7 45.2 reduce-scatter.4
where the time goes:
time: 1290 us
  waiting for transfers between devices  1200 us (93%)
  blocking collectives  45.9 us (4%)
  matrix products  14.1 us (1%)
  between operations  13.9 us (1%)
    reduce_scatter x1, waiting for transfers between devices, on_device(): lax.psum_scatter(contract_first(logit_cot, query_unit_vectors), 'dp', sca...  753 us
    unnamed x5, waiting for transfers between devices  254 us
    all_gather x1, waiting for transfers between devices, on_device(): lax.all_gather(candidate_unit_vectors, 'dp', axis=0, tiled=True)  149 us
    reduce_scatter x1, waiting for transfers between devices, on_device(): lax.psum_scatter(dense_rows.astype(jnp.bfloat16), 'grp', scatter_dimensio...  46.5 us
  transfers between devices with their start and end apart: 4, of which 4 were waited for; matrix products, arithmetic and copies ran while one was open for 0% of the time, Pallas kernels for 0%

commit v1 on v0

v1 whole, which is shorter than its diff:
```python
import jax
import jax.numpy as jnp
from jax import lax
from jax.experimental import pallas as pl
from jax.experimental.pallas import tpu as pltpu
from jax.sharding import Mesh, PartitionSpec as P

TOUCH = 64
NZ, NY, NX, NC = 16, 8, 4, 2
ITEMS = 32
EMB = 256
W = 256
H = 1024
GROUP = ITEMS * NX * NC
HALF = GROUP // NC
USERS = NY * GROUP
SCORE_BLOCK = 256
META = 128
FACT = EMB + W + META

inv_temperature = 1.0 / 0.02
epsilon = 1e-06
f32, bf16 = jnp.float32, jnp.bfloat16


def nn(left, right):
    return lax.dot_general(left, right, (((1,), (0,)), ((), ())), preferred_element_type=f32)


def nt(left, right):
    return lax.dot_general(left, right, (((1,), (1,)), ((), ())), preferred_element_type=f32)


def tn(left, right):
    return lax.dot_general(left, right, (((0,), (0,)), ((), ())), preferred_element_type=f32)


def unit_rows(values):
    return values * lax.rsqrt(jnp.sum(values * values, axis=-1, keepdims=True) + epsilon)


def call(body, outs, args, flops, grid=None, in_specs=None, out_specs=None, scratch=(), exps=0):
    moved = sum(a.size * a.dtype.itemsize for a in args)
    moved += sum(o.size * o.dtype.itemsize for o in outs)
    extra = {} if grid is None else dict(grid=grid, in_specs=in_specs, out_specs=out_specs)
    return pl.pallas_call(
        body,
        out_shape=outs,
        scratch_shapes=list(scratch),
        cost_estimate=pl.CostEstimate(flops=flops, bytes_accessed=moved, transcendentals=exps),
        compiler_params=pltpu.CompilerParams(vmem_limit_bytes=24 * 1024 * 1024),
        **extra,
    )(*args)


def shape(dims, kind):
    return jax.ShapeDtypeStruct(dims, kind)


def user_kernel(me_ref, user_hbm, spread_ref, positive_ref, half_ref, own_ref, sems):
    core = lax.rem(me_ref[0], NC)
    half = pl.ds(pl.multiple_of(core * HALF, HALF), HALF)
    own = pl.ds(pl.multiple_of(me_ref[0] * ITEMS, ITEMS), ITEMS)
    half_copy = pltpu.make_async_copy(user_hbm.at[half], half_ref, sems.at[0])
    own_copy = pltpu.make_async_copy(user_hbm.at[own], own_ref, sems.at[1])
    half_copy.start()
    own_copy.start()
    half_copy.wait()
    unit = unit_rows(half_ref[...].astype(f32)).astype(bf16)
    for peer in range(NY):
        spread_ref[peer] = unit
    own_copy.wait()
    positive_ref[...] = unit_rows(own_ref[...].astype(f32)).astype(bf16)


def tower_kernel(
    emb_ref, w_one_ref, w_two_ref, owner_ref, slot_ref, spread_ref, dir_ref, scale_ref, base_ref
):
    emb = emb_ref[...]
    pair = lax.broadcasted_iota(jnp.int32, (2, META), 0)
    lane = lax.broadcasted_iota(jnp.int32, (2, META), 1)
    at_owner = jnp.where(lane == 2 * pair, 1.0, 0.0)
    at_slot = jnp.where(lane == 2 * pair + 1, 1.0, 0.0)
    meta = tn(owner_ref[...].astype(f32), at_owner) + tn(slot_ref[...].astype(f32), at_slot)
    base_ref[:, :EMB] = emb
    base_ref[:, EMB:] = meta.astype(bf16)
    preact = nn(emb, w_one_ref[...])
    hidden = (preact * jax.nn.sigmoid(preact)).astype(bf16)
    item_out = nn(hidden, w_two_ref[...])
    scale = lax.rsqrt(jnp.sum(item_out * item_out, axis=1, keepdims=True) + epsilon)
    item_dir = item_out * scale
    unit = item_dir.astype(bf16)
    for peer in range(NZ):
        spread_ref[peer] = unit
    dir_ref[...] = item_dir
    scale_ref[...] = jnp.broadcast_to(scale, (ITEMS, 128))


def score_kernel(items_ref, own_ref, other_ref, powers_ref, spread_ref, sums_ref):
    items = items_ref[...]
    for step in range(USERS // SCORE_BLOCK):
        users_ref = own_ref if step < USERS // SCORE_BLOCK // 2 else other_ref
        first = step * SCORE_BLOCK % (USERS // 2)
        scores = nt(items, users_ref[first : first + SCORE_BLOCK, :]) * inv_temperature
        powers = jnp.exp(scores)
        first = step * SCORE_BLOCK
        powers_ref[:, first : first + SCORE_BLOCK] = powers.astype(bf16)
        sums = jnp.sum(powers, axis=0, keepdims=True)
        for k in range(SCORE_BLOCK // 128):
            row = first // 128 + k
            sums_ref[row : row + 1, :] = sums[:, k * 128 : (k + 1) * 128]
    spread_ref[...] = jnp.broadcast_to(sums_ref[...].astype(bf16)[None], spread_ref.shape)


def unit_cot_kernel(me_ref, parts_ref, own_ref, other_ref, powers_ref, out_ref, scaled_ref):
    half = USERS // 128 // 2
    core = lax.rem(me_ref[0], NC)
    mine = parts_ref[core].astype(f32)
    theirs = parts_ref[1 - core].astype(f32)
    for peer in range(1, NY * NX):
        mine += parts_ref[NC * peer + core].astype(f32)
        theirs += parts_ref[NC * peer + 1 - core].astype(f32)
    totals = mine + jnp.concatenate([theirs[half:], theirs[:half]], axis=0)
    inverse = jnp.transpose(1.0 / totals)
    for k in range(USERS // 128):
        users_ref = own_ref if k < half else other_ref
        first = k % half * 128
        block = users_ref[first : first + 128, :].astype(f32) * inverse[:, k : k + 1]
        scaled_ref[k * 128 : (k + 1) * 128, :] = block.astype(bf16)
    out_ref[...] = nn(powers_ref[...], scaled_ref[...]).astype(bf16)


def cot_kernel(parts_ref, positive_ref, dir_ref, scale_ref, base_ref, spread_ref):
    unit_cot = parts_ref[0].astype(f32)
    for peer in range(1, NZ):
        unit_cot += parts_ref[peer].astype(f32)
    unit_cot -= positive_ref[...].astype(f32)
    item_dir = dir_ref[...]
    along = jnp.sum(item_dir * unit_cot, axis=1, keepdims=True)
    out_cot = ((unit_cot - item_dir * along) * scale_ref[:, :1]).astype(bf16)
    base = base_ref[...]
    for peer in range(NX):
        spread_ref[peer, :, : EMB + META] = base
        spread_ref[peer, :, EMB + META :] = out_cot


def grads_kernel(me_ref, fact_ref, w_one_ref, w_two_ref, table_ref, part_ref):
    me = me_ref[0]
    emb = fact_ref[:, :EMB]
    meta = fact_ref[:, EMB : EMB + META].astype(f32)
    cot = fact_ref[:, EMB + META :]
    w_one = w_one_ref[...]
    preact = nn(emb, w_one)
    sig = jax.nn.sigmoid(preact)
    hidden = (preact * sig).astype(bf16)
    slopes = sig * (1.0 + preact * (1.0 - sig))
    preact_cot = (nt(cot, w_two_ref[...]) * slopes).astype(bf16)
    emb_cot = nt(preact_cot, w_one)
    mine = me.astype(f32)
    slots = lax.broadcasted_iota(jnp.int32, (GROUP, TOUCH), 1).astype(f32)
    placing = jnp.where((meta[:, 0:1] == mine) & (meta[:, 1:2] == slots), 1.0, 0.0)
    placing += jnp.where((meta[:, 2:3] == mine) & (meta[:, 3:4] == slots), 1.0, 0.0)
    table_ref[...] = tn(placing.astype(bf16), emb_cot.astype(bf16))
    count = H // (NX * NC)
    unit = lax.broadcasted_iota(jnp.int32, (H, count), 0)
    column = lax.broadcasted_iota(jnp.int32, (H, count), 1)
    pick = jnp.where(unit == column * (NX * NC) + me, 1.0, 0.0).astype(bf16)
    part_ref[:, 0, :] = tn(nn(preact_cot, pick).astype(bf16), emb).astype(bf16)
    part_ref[:, 1, :] = tn(nn(hidden, pick).astype(bf16), cot).astype(bf16)


def gather_pair(values):
    return lax.all_gather(values, "c", axis=0, tiled=True)


def trade_pair(values):
    return lax.ppermute(values, "c", [(0, 1), (1, 0)])


def on_device(user_vec, item_emb, w_one, w_two, item_owner, item_slot):
    me = lax.axis_index("x") * NC + lax.axis_index("c")
    place = me.reshape(1)
    vmem = pl.BlockSpec(memory_space=pltpu.VMEM)
    smem = pl.BlockSpec(memory_space=pltpu.SMEM)
    hbm = pl.BlockSpec(memory_space=pltpu.HBM)
    user_spread, positive = call(
        user_kernel,
        (shape((NY, HALF, W), bf16), shape((ITEMS, W), bf16)),
        (place, user_vec),
        4 * HALF * W,
        grid=(),
        in_specs=[smem, hbm],
        out_specs=(vmem, vmem),
        scratch=(
            pltpu.VMEM((HALF, W), bf16),
            pltpu.VMEM((ITEMS, W), bf16),
            pltpu.SemaphoreType.DMA((2,)),
        ),
    )
    users = lax.all_to_all(user_spread, "y", 0, 0)
    users = users.reshape(NY * HALF, W)
    others = trade_pair(users)
    item_spread, item_dir, item_scale, base = call(
        tower_kernel,
        (
            shape((NZ, ITEMS, W), bf16),
            shape((ITEMS, W), f32),
            shape((ITEMS, 128), f32),
            shape((ITEMS, EMB + META), bf16),
        ),
        (item_emb, w_one, w_two, item_owner.T, item_slot.T),
        4 * ITEMS * EMB * H,
    )
    count = NZ * ITEMS
    items = lax.all_to_all(item_spread, "z", 0, 0).reshape(count, W)
    powers, sums = call(
        score_kernel,
        (shape((count, USERS), bf16), shape((NY * NX * NC, USERS // 128, 128), bf16)),
        (items, users, others),
        2 * count * USERS * W,
        scratch=(pltpu.VMEM((USERS // 128, 128), f32),),
        exps=count * USERS,
    )
    sums = lax.all_to_all(sums, ("y", "x", "c"), 0, 0)
    partial = call(
        unit_cot_kernel,
        (shape((count, W), bf16),),
        (place, sums, users, others, powers),
        2 * count * USERS * W,
        grid=(),
        in_specs=[smem, vmem, vmem, vmem, vmem],
        out_specs=(vmem,),
        scratch=(pltpu.VMEM((USERS, W), bf16),),
    )[0]
    parts = lax.all_to_all(partial.reshape(NZ, ITEMS, W), "z", 0, 0)
    facts = call(
        cot_kernel,
        (shape((NX, ITEMS, FACT), bf16),),
        (parts, positive, item_dir, item_scale, base),
        NZ * ITEMS * W,
    )[0]
    facts = gather_pair(lax.all_to_all(facts, "x", 0, 0).reshape(NX * ITEMS, FACT))
    table_grad, part = call(
        grads_kernel,
        (shape((TOUCH, EMB), f32), shape((H // (NX * NC), 2, W), bf16)),
        (place, facts, w_one, w_two),
        2 * GROUP * EMB * H * 5,
        grid=(),
        in_specs=[smem, vmem, vmem, vmem],
        out_specs=(vmem, vmem),
    )
    part = lax.all_to_all(part, ("z", "y"), 0, 0, tiled=True)
    w_grads = jnp.sum(part.astype(f32), axis=0).reshape(1, EMB + W)
    return (table_grad, w_grads)


def solution(mesh):
    fine = Mesh(mesh.devices.reshape(NZ, NY, NX, NC), ("z", "y", "x", "c"))
    dp, every = ("z", "y"), ("z", "y", "x", "c")
    placed = (P(dp, None), P(every, None), P(), P(), P(every, None), P(every, None))
    return jax.shard_map(
        on_device,
        mesh=fine,
        in_specs=placed,
        out_specs=(P(every, None), P(every, None)),
        check_vma=False,
    )
```

time: 1290 us -> 149 us (0.12)
  waiting for transfers between devices: 1200 us -> 17.7 us
  blocking collectives: 45.9 us -> 82.2 us
  starting transfers between devices: 0.16 us -> 34.7 us
  matrix products: 14.1 us -> 0 us
  between operations: 13.9 us -> 0.71 us
    reduce_scatter x2 -> x0, waiting for transfers between devices: 800 us -> none  [the longest x1 753 us: on_device(): lax.psum_scatter(contract_first(logit_cot, query_unit_vectors), 'dp', sca...]
    unnamed x5 -> x0, waiting for transfers between devices: 254 us -> none
    all_gather x1 -> x0, waiting for transfers between devices: 149 us -> none  [on_device(): lax.all_gather(candidate_unit_vectors, 'dp', axis=0, tiled=True)]
    all_to_all x0 -> x4, blocking collectives: none -> 73.8 us  [the longest x1 23.6 us: on_device(): part = lax.all_to_all(part, ('z', 'y'), 0, 0, tiled=True)]
    all_to_all x0 -> x2, starting transfers between devices: none -> 32.1 us  [the longest x1 24.4 us: on_device(): items = lax.all_to_all(item_spread, 'z', 0, 0).reshape(count, W)]
    psum x1 -> x0, blocking collectives: 21.4 us -> none  [on_device(): totals = lax.psum(jnp.sum(powers, axis=1), 'grp')]
    all_to_all x0 -> x2, waiting for transfers between devices: none -> 17.7 us  [the longest x1 11 us: on_device(): items = lax.all_to_all(item_spread, 'z', 0, 0).reshape(count, W)]
    all_gather x1, blocking collectives: 24.5 us -> 8.33 us  [gather_pair(): return lax.all_gather(values, 'c', axis=0, tiled=True)]
  transfers between devices with their start and end apart: 4 -> 3, of which waited for: 4 -> 2; matrix products, arithmetic and copies ran while one was open for 0% -> 0% of each run, Pallas kernels for 0% -> 1%
where the time goes in v1:
time: 149 us; the launch traced here: 147 us
  blocking collectives  82.2 us (55%)
  starting transfers between devices  34.7 us (23%)
  waiting for transfers between devices  17.7 us (12%)
  Pallas kernels  6.1 us (4%)
  local copies, waits for them, and re-layouts  5.64 us (4%)
    all_to_all x1, starting transfers between devices, on_device(): items = lax.all_to_all(item_spread, 'z', 0, 0).reshape(count, W)  24.4 us
    all_to_all x1, blocking collectives, on_device(): part = lax.all_to_all(part, ('z', 'y'), 0, 0, tiled=True)  23.6 us
    all_to_all x1, blocking collectives, on_device(): sums = lax.all_to_all(sums, ('y', 'x', 'c'), 0, 0)  23.3 us
    all_to_all x1, blocking collectives, on_device(): parts = lax.all_to_all(partial.reshape(NZ, ITEMS, W), 'z', 0, 0)  19.6 us
    all_to_all x1, waiting for transfers between devices, on_device(): items = lax.all_to_all(item_spread, 'z', 0, 0).reshape(count, W)  11 us
    all_gather x1, blocking collectives, gather_pair(): return lax.all_gather(values, 'c', axis=0, tiled=True)  8.33 us
    all_to_all x1, starting transfers between devices, on_device(): users = lax.all_to_all(user_spread, 'y', 0, 0)  7.66 us
    all_to_all x1, blocking collectives, on_device(): lax.all_to_all(facts, 'x', 0, 0).reshape(NX * ITEMS, FACT)  7.36 us
  transfers between devices with their start and end apart: 3, of which 2 were waited for; matrix products, arithmetic and copies ran while one was open for 0% of the time, Pallas kernels for 1%

profile of v1, /device:TPU:1, one launch (start us, length us, event | category | flops | bytes accessed | tf_op | source)
XLA Modules:
  0.0 147.3 jit_solution(9967416044279025935)
XLA Ops:
  0.6 0.0 copy-start.4
  0.6 0.9 copy-done.4
  1.5 1.0 shard_map.78
  2.6 7.7 %all-to-all-start.1 = ((bf16[8,128,256]{2,1,0:T(8,128)(2,1)}), bf16[8,128,256]{2,1,0:T(8,128)(2,1)S(1)}, u32[]{:S(2)}, u32[]{:S(2)}) async-start(bf16[8,128,256]{2,1,0:T(8,128)(2,1)} %get-tuple-element.13), calls=%async_computation.1 | async-start | bytes 1048576 | tf_op jit(solution)/shard_map/all_to_all | solution.py:200
  10.2 0.0 copy-start
  10.2 1.0 copy-done
  11.3 0.0 copy-start.2
  11.3 1.0 copy-done.2
  12.3 0.0 copy-start.5
  12.3 0.7 copy-done.5
  13.0 0.0 copy-start.6
  13.0 0.7 copy-done.6
  13.7 0.0 copy-start.7
  13.7 0.7 copy-done.7
  14.4 1.3 shard_map.77
  15.7 6.7 %all-to-all-done.1 = bf16[8,128,256]{2,1,0:T(8,128)(2,1)S(1)} async-done(((bf16[8,128,256]{2,1,0:T(8,128)(2,1)}), bf16[8,128,256]{2,1,0:T(8,128)(2,1)S(1)}, u32[]{:S(2)}, u32[]{:S(2)}) %all-to-all-start.1) | async-done | bytes 524320 | tf_op jit(solution)/shard_map/all_to_all | solution.py:200
  22.4 24.4 %all-to-all-start = ((bf16[16,32,256]{2,1,0:T(8,128)(2,1)}), bf16[16,32,256]{2,1,0:T(8,128)(2,1)S(1)}, u32[]{:S(2)}, u32[]{:S(2)}) async-start(bf16[16,32,256]{2,1,0:T(8,128)(2,1)} %get-tuple-element.12), calls=%async_computation | async-start | bytes 524288 | tf_op jit(solution)/shard_map/all_to_all | solution.py:215
  46.8 2.7 %collective-permute-start = (bf16[1024,256]{1,0:T(8,128)(2,1)S(1)}, bf16[1024,256]{1,0:T(8,128)(2,1)S(1)}, u32[]{:S(2)}, u32[]{:S(2)}) collective-permute-start(bf16[1024,256]{1,0:T(8,128)(2,1)S(1)} %bitcast.10), channel_id=1, source_target_pairs={{0,1},{1,0},{2,3},{3,2},{4,5},{5,4},{6,7},{7,6},{8,9},{9,8},{10,11... | collective-permute-start | bytes 1572872 | tf_op jit(solution)/shard_map/ppermute | solution.py:177
  49.5 11.0 %all-to-all-done = bf16[16,32,256]{2,1,0:T(8,128)(2,1)S(1)} async-done(((bf16[16,32,256]{2,1,0:T(8,128)(2,1)}), bf16[16,32,256]{2,1,0:T(8,128)(2,1)S(1)}, u32[]{:S(2)}, u32[]{:S(2)}) %all-to-all-start) | async-done | bytes 262176 | tf_op jit(solution)/shard_map/all_to_all | solution.py:215
  60.5 0.0 collective-permute-done.other_ref
  60.5 0.9 shard_map.79
  61.4 23.3 %all_to_all.30.parts_ref = bf16[64,16,128]{2,1,0:T(8,128)(2,1)S(1)} all-to-all(bf16[64,16,128]{2,1,0:T(8,128)(2,1)S(1)} %get-tuple-element.14), channel_id=1, replica_groups=mesh['z'=16,'y'=8,'x'=4,'c'=2] {'y','x','c'}, dimensions={0} | all-to-all | bytes 524288 | tf_op jit(solution)/shard_map/all_to_all | solution.py:224
  84.6 0.0 copy-start.1
  84.6 0.0 copy-start.3
  84.6 1.0 shard_map.80
  85.7 19.6 %all_to_all.31.parts_ref = bf16[16,32,256]{2,1,0:T(8,128)(2,1)S(1)} all-to-all(bf16[16,32,256]{2,1,0:T(8,128)(2,1)S(1)} %bitcast.13), channel_id=1, replica_groups=mesh['z'=16,'y'=8,'x'=4,'c'=2] {'z'}, dimensions={0} | all-to-all | bytes 524288 | tf_op jit(solution)/shard_map/all_to_all | solution.py:235
  105.2 0.1 shard_map.81
  105.3 7.4 %all_to_all.32 = bf16[4,32,640]{2,1,0:T(8,128)(2,1)S(1)} all-to-all(bf16[4,32,640]{2,1,0:T(8,128)(2,1)S(1)} %shard_map.81), channel_id=1, replica_groups=mesh['z'=16,'y'=8,'x'=4,'c'=2] {'x'}, dimensions={0} | all-to-all | bytes 327680 | tf_op jit(solution)/shard_map/all_to_all | solution.py:242
  112.7 8.3 %all_gather.3.fact_ref = bf16[256,640]{1,0:T(8,128)(2,1)S(1)} all-gather(bf16[128,640]{1,0:T(8,128)(2,1)S(1)} %bitcast.17), channel_id=1, replica_groups=mesh['z'=16,'y'=8,'x'=4,'c'=2] {'c'}, dimensions={0}, use_global_device_ids=true | all-gather | bytes 491520 | tf_op jit(solution)/shard_map/all_gather | solution.py:173
  121.0 0.0 copy-done.1
  121.0 0.0 copy-done.3
  121.0 1.8 %shard_map.82 = (f32[64,256]{1,0:T(8,128)}, bf16[128,2,256]{2,1,0:T(2,128)(2,1)S(1)}) custom-call(s32[1]{0:T(128)} %bitcast.me_ref, bf16[256,640]{1,0:T(8,128)(2,1)S(1)} %all_gather.3.fact_ref, bf16[256,1024]{1,0:T(8,128)(2,1)S(1)} %copy-done.1, bf16[1024,256]{1,0:T(8,128)(2,1)S(1)} %copy-done.3), custom_call_target="tpu_custom_call" | custom-call | flops 671088640 | bytes 1572868 | tf_op jit(solution)/shard_map/pallas_call | solution.py:46
  122.9 23.6 %all_to_all.33 = bf16[128,2,256]{2,1,0:T(2,128)(2,1)S(1)} all-to-all(bf16[128,2,256]{2,1,0:T(2,128)(2,1)S(1)} %get-tuple-element.21), channel_id=1, replica_groups=mesh['z'=16,'y'=8,'x'=4,'c'=2] {'z','y'}, dimensions={0} | all-to-all | bytes 262144 | tf_op jit(solution)/shard_map/all_to_all | solution.py:252
  146.5 0.2 convert_reduce_fusion
  146.7 0.6 copy.8
Async XLA Ops:
  0.6 0.9 copy-start.4
  2.6 19.8 %all-to-all-start.1 = ((bf16[8,128,256]{2,1,0:T(8,128)(2,1)}), bf16[8,128,256]{2,1,0:T(8,128)(2,1)S(1)}, u32[]{:S(2)}, u32[]{:S(2)}) async-start(bf16[8,128,256]{2,1,0:T(8,128)(2,1)} %get-tuple-element.13), calls=%async_computation.1 | async-start | bytes 1048576 | tf_op jit(solution)/shard_map/all_to_all | solution.py:200
  10.2 1.0 copy-start
  11.3 1.0 copy-start.2
  12.3 0.7 copy-start.5
  13.0 0.7 copy-start.6
  13.7 0.7 copy-start.7
  22.4 38.1 %all-to-all-start = ((bf16[16,32,256]{2,1,0:T(8,128)(2,1)}), bf16[16,32,256]{2,1,0:T(8,128)(2,1)S(1)}, u32[]{:S(2)}, u32[]{:S(2)}) async-start(bf16[16,32,256]{2,1,0:T(8,128)(2,1)} %get-tuple-element.12), calls=%async_computation | async-start | bytes 524288 | tf_op jit(solution)/shard_map/all_to_all | solution.py:215
  46.8 13.7 %collective-permute-start = (bf16[1024,256]{1,0:T(8,128)(2,1)S(1)}, bf16[1024,256]{1,0:T(8,128)(2,1)S(1)}, u32[]{:S(2)}, u32[]{:S(2)}) collective-permute-start(bf16[1024,256]{1,0:T(8,128)(2,1)S(1)} %bitcast.10), channel_id=1, source_target_pairs={{0,1},{1,0},{2,3},{3,2},{4,5},{5,4},{6,7},{7,6},{8,9},{9,8},{10,11... | collective-permute-start | bytes 1572872 | tf_op jit(solution)/shard_map/ppermute | solution.py:177
  84.6 36.4 %copy-start.1 = (bf16[256,1024]{1,0:T(8,128)(2,1)S(1)}, bf16[256,1024]{1,0:T(8,128)(2,1)}, u32[]{:S(2)}) copy-start(bf16[256,1024]{1,0:T(8,128)(2,1)} %w_one_ref.3) | copy-start | bytes 1572868
  84.6 36.4 %copy-start.3 = (bf16[1024,256]{1,0:T(8,128)(2,1)S(1)}, bf16[1024,256]{1,0:T(8,128)(2,1)}, u32[]{:S(2)}) copy-start(bf16[1024,256]{1,0:T(8,128)(2,1)} %w_two_ref.3) | copy-start | bytes 1572868

commit v2 on v1

--- a/solution.py
+++ b/solution.py
@@ -15,6 +15,7 @@
 HALF = GROUP // NC
 USERS = NY * GROUP
 SCORE_BLOCK = 256
+LARGE = 63 * 1024 * 1024 + 512 * 1024
 META = 128
 FACT = EMB + W + META
 
@@ -39,7 +40,7 @@
     return values * lax.rsqrt(jnp.sum(values * values, axis=-1, keepdims=True) + epsilon)
 
 
-def call(body, outs, args, flops, grid=None, in_specs=None, out_specs=None, scratch=(), exps=0):
+def call(body, outs, args, flops, grid=None, in_specs=None, out_specs=None, scratch=(), exps=0, vmem=24 * 1024 * 1024):
     moved = sum(a.size * a.dtype.itemsize for a in args)
     moved += sum(o.size * o.dtype.itemsize for o in outs)
     extra = {} if grid is None else dict(grid=grid, in_specs=in_specs, out_specs=out_specs)
@@ -48,7 +49,7 @@
         out_shape=outs,
         scratch_shapes=list(scratch),
         cost_estimate=pl.CostEstimate(flops=flops, bytes_accessed=moved, transcendentals=exps),
-        compiler_params=pltpu.CompilerParams(vmem_limit_bytes=24 * 1024 * 1024),
+        compiler_params=pltpu.CompilerParams(vmem_limit_bytes=vmem),
         **extra,
     )(*args)
 
@@ -96,7 +97,7 @@
     scale_ref[...] = jnp.broadcast_to(scale, (ITEMS, 128))
 
 
-def score_kernel(items_ref, own_ref, other_ref, powers_ref, spread_ref, sums_ref):
+def score_kernel(items_ref, own_ref, other_ref, powers_ref, sums_ref):
     items = items_ref[...]
     for step in range(USERS // SCORE_BLOCK):
         users_ref = own_ref if step < USERS // SCORE_BLOCK // 2 else other_ref
@@ -109,18 +110,20 @@
         for k in range(SCORE_BLOCK // 128):
             row = first // 128 + k
             sums_ref[row : row + 1, :] = sums[:, k * 128 : (k + 1) * 128]
-    spread_ref[...] = jnp.broadcast_to(sums_ref[...].astype(bf16)[None], spread_ref.shape)
-
-
-def unit_cot_kernel(me_ref, parts_ref, own_ref, other_ref, powers_ref, out_ref, scaled_ref):
+
+
+def pair_kernel(mine_ref, theirs_ref, spread_ref):
     half = USERS // 128 // 2
-    core = lax.rem(me_ref[0], NC)
-    mine = parts_ref[core].astype(f32)
-    theirs = parts_ref[1 - core].astype(f32)
+    theirs = theirs_ref[...]
+    total = mine_ref[...] + jnp.concatenate([theirs[half:], theirs[:half]], axis=0)
+    spread_ref[...] = jnp.broadcast_to(total.astype(bf16)[None], spread_ref.shape)
+
+
+def unit_cot_kernel(parts_ref, own_ref, other_ref, powers_ref, out_ref, scaled_ref):
+    half = USERS // 128 // 2
+    totals = parts_ref[0].astype(f32)
     for peer in range(1, NY * NX):
-        mine += parts_ref[NC * peer + core].astype(f32)
-        theirs += parts_ref[NC * peer + 1 - core].astype(f32)
-    totals = mine + jnp.concatenate([theirs[half:], theirs[:half]], axis=0)
+        totals += parts_ref[peer].astype(f32)
     inverse = jnp.transpose(1.0 / totals)
     for k in range(USERS // 128):
         users_ref = own_ref if k < half else other_ref
@@ -196,6 +199,7 @@
             pltpu.VMEM((ITEMS, W), bf16),
             pltpu.SemaphoreType.DMA((2,)),
         ),
+        vmem=LARGE,
     )
     users = lax.all_to_all(user_spread, "y", 0, 0)
     users = users.reshape(NY * HALF, W)
@@ -215,21 +219,23 @@
     items = lax.all_to_all(item_spread, "z", 0, 0).reshape(count, W)
     powers, sums = call(
         score_kernel,
-        (shape((count, USERS), bf16), shape((NY * NX * NC, USERS // 128, 128), bf16)),
+        (shape((count, USERS), bf16), shape((USERS // 128, 128), f32)),
         (items, users, others),
         2 * count * USERS * W,
-        scratch=(pltpu.VMEM((USERS // 128, 128), f32),),
         exps=count * USERS,
     )
-    sums = lax.all_to_all(sums, ("y", "x", "c"), 0, 0)
+    sums = call(
+        pair_kernel,
+        (shape((NY * NX, USERS // 128, 128), bf16),),
+        (sums, trade_pair(sums)),
+        USERS,
+    )[0]
+    sums = lax.all_to_all(sums, ("y", "x"), 0, 0)
     partial = call(
         unit_cot_kernel,
         (shape((count, W), bf16),),
-        (place, sums, users, others, powers),
+        (sums, users, others, powers),
         2 * count * USERS * W,
-        grid=(),
-        in_specs=[smem, vmem, vmem, vmem, vmem],
-        out_specs=(vmem,),
         scratch=(pltpu.VMEM((USERS, W), bf16),),
     )[0]
     parts = lax.all_to_all(partial.reshape(NZ, ITEMS, W), "z", 0, 0)

time: 149 us -> 148 us (level)
  blocking collectives: 82.2 us -> 72.8 us
  starting transfers between devices: 34.7 us -> 42.1 us
    all_to_all x1, blocking collectives: 23.3 us -> 13.6 us  [on_device(): sums = lax.all_to_all(sums, ('y', 'x'), 0, 0)]
    ppermute x1 -> x2, starting transfers between devices: 2.68 us -> 10 us  [trade_pair(): return lax.ppermute(values, 'c', [(0, 1), (1, 0)])]
    all_gather x1, blocking collectives: 8.33 us -> 9.95 us  [gather_pair(): return lax.all_gather(values, 'c', axis=0, tiled=True)]
    pallas_call x6 -> x7, Pallas kernels: 6.1 us -> 6.83 us  [call(): pl.pallas_call(body, out_shape=outs, scratch_shapes=list(scratch), cost_e...]
  transfers between devices with their start and end apart: 3 -> 4, of which waited for: 2 -> 3; matrix products, arithmetic and copies ran while one was open for 0% -> 0% of each run, Pallas kernels for 1% -> 1%
where the time goes in v2:
time: 148 us; the launch traced here: 146 us
  blocking collectives  72.8 us (49%)
  starting transfers between devices  42.1 us (28%)
  waiting for transfers between devices  18.5 us (12%)
  Pallas kernels  6.83 us (5%)
  local copies, waits for them, and re-layouts  4.75 us (3%)
    all_to_all x1, starting transfers between devices, on_device(): items = lax.all_to_all(item_spread, 'z', 0, 0).reshape(count, W)  24.4 us
    all_to_all x1, blocking collectives, on_device(): part = lax.all_to_all(part, ('z', 'y'), 0, 0, tiled=True)  23.7 us
    all_to_all x1, blocking collectives, on_device(): parts = lax.all_to_all(partial.reshape(NZ, ITEMS, W), 'z', 0, 0)  18.2 us
    all_to_all x1, blocking collectives, on_device(): sums = lax.all_to_all(sums, ('y', 'x'), 0, 0)  13.6 us
    all_to_all x1, waiting for transfers between devices, on_device(): items = lax.all_to_all(item_spread, 'z', 0, 0).reshape(count, W)  11 us
    ppermute x2, starting transfers between devices, trade_pair(): return lax.ppermute(values, 'c', [(0, 1), (1, 0)])  10 us
    all_gather x1, blocking collectives, gather_pair(): return lax.all_gather(values, 'c', axis=0, tiled=True)  9.95 us
    all_to_all x1, starting transfers between devices, on_device(): users = lax.all_to_all(user_spread, 'y', 0, 0)  7.66 us
  transfers between devices with their start and end apart: 4, of which 3 were waited for; matrix products, arithmetic and copies ran while one was open for 0% of the time, Pallas kernels for 1%

profile of v2, /device:TPU:1, one launch (start us, length us, event | category | flops | bytes accessed | tf_op | source)
XLA Modules:
  0.0 145.9 jit_solution(9462761704186213157)
XLA Ops:
  0.6 1.8 %shard_map.78 = (bf16[8,128,256]{2,1,0:T(8,128)(2,1)}, bf16[32,256]{1,0:T(8,128)(2,1)}) custom-call(s32[1]{0:T(128)} %bitcast.me_ref, bf16[256,256]{1,0:T(8,128)(2,1)} %user_hbm.1), custom_call_target="tpu_custom_call" | custom-call | flops 131072 | bytes 671748 | tf_op jit(solution)/shard_map/pallas_call | solution.py:47
  2.4 7.7 %all-to-all-start.1 = ((bf16[8,128,256]{2,1,0:T(8,128)(2,1)}), bf16[8,128,256]{2,1,0:T(8,128)(2,1)S(1)}, u32[]{:S(2)}, u32[]{:S(2)}) async-start(bf16[8,128,256]{2,1,0:T(8,128)(2,1)} %get-tuple-element.13), calls=%async_computation.1 | async-start | bytes 1048576 | tf_op jit(solution)/shard_map/all_to_all | solution.py:204
  10.1 0.0 copy-start
  10.1 1.0 copy-done
  11.1 0.0 copy-start.2
  11.1 1.0 copy-done.2
  12.2 0.0 copy-start.4
  12.2 0.7 copy-done.4
  12.9 0.0 copy-start.6
  12.9 0.7 copy-done.6
  13.6 0.0 copy-start.7
  13.6 0.7 copy-done.7
  14.2 1.3 shard_map.77
  15.5 6.7 %all-to-all-done.1 = bf16[8,128,256]{2,1,0:T(8,128)(2,1)S(1)} async-done(((bf16[8,128,256]{2,1,0:T(8,128)(2,1)}), bf16[8,128,256]{2,1,0:T(8,128)(2,1)S(1)}, u32[]{:S(2)}, u32[]{:S(2)}) %all-to-all-start.1) | async-done | bytes 524320 | tf_op jit(solution)/shard_map/all_to_all | solution.py:204
  22.2 24.4 %all-to-all-start = ((bf16[16,32,256]{2,1,0:T(8,128)(2,1)}), bf16[16,32,256]{2,1,0:T(8,128)(2,1)S(1)}, u32[]{:S(2)}, u32[]{:S(2)}) async-start(bf16[16,32,256]{2,1,0:T(8,128)(2,1)} %get-tuple-element.12), calls=%async_computation | async-start | bytes 524288 | tf_op jit(solution)/shard_map/all_to_all | solution.py:219
  46.6 2.7 %collective-permute-start = (bf16[1024,256]{1,0:T(8,128)(2,1)S(1)}, bf16[1024,256]{1,0:T(8,128)(2,1)S(1)}, u32[]{:S(2)}, u32[]{:S(2)}) collective-permute-start(bf16[1024,256]{1,0:T(8,128)(2,1)S(1)} %bitcast.10), channel_id=1, source_target_pairs={{0,1},{1,0},{2,3},{3,2},{4,5},{5,4},{6,7},{7,6},{8,9},{9,8},{10,11... | collective-permute-start | bytes 1572872 | tf_op jit(solution)/shard_map/ppermute | solution.py:180
  49.3 11.0 %all-to-all-done = bf16[16,32,256]{2,1,0:T(8,128)(2,1)S(1)} async-done(((bf16[16,32,256]{2,1,0:T(8,128)(2,1)}), bf16[16,32,256]{2,1,0:T(8,128)(2,1)S(1)}, u32[]{:S(2)}, u32[]{:S(2)}) %all-to-all-start) | async-done | bytes 262176 | tf_op jit(solution)/shard_map/all_to_all | solution.py:219
  60.4 0.0 collective-permute-done.other_ref
  60.4 0.9 shard_map.79
  61.2 7.4 %collective-permute-start.1 = (f32[16,128]{1,0:T(8,128)S(1)}, f32[16,128]{1,0:T(8,128)S(1)}, u32[]{:S(2)}, u32[]{:S(2)}) collective-permute-start(f32[16,128]{1,0:T(8,128)S(1)} %get-tuple-element.14.mine_ref), channel_id=1, source_target_pairs={{0,1},{1,0},{2,3},{3,2},{4,5},{5,4},{6,7},{7,6},{8,9},{9,8},{10,11... | collective-permute-start | bytes 24584 | tf_op jit(solution)/shard_map/ppermute | solution.py:180
  68.6 0.8 collective-permute-done.1.theirs_ref
  69.4 13.6 %all_to_all.30.parts_ref = bf16[32,16,128]{2,1,0:T(8,128)(2,1)S(1)} all-to-all(bf16[32,16,128]{2,1,0:T(8,128)(2,1)S(1)} %shard_map.80), channel_id=1, replica_groups=mesh['z'=16,'y'=8,'x'=4,'c'=2] {'y','x'}, dimensions={0} | all-to-all | bytes 262144 | tf_op jit(solution)/shard_map/all_to_all | solution.py:233
  83.0 0.0 copy-start.5
  83.0 0.0 copy-start.1
  83.0 0.0 copy-start.3
  83.0 1.0 shard_map.81
  84.0 18.2 %all_to_all.31.parts_ref = bf16[16,32,256]{2,1,0:T(8,128)(2,1)S(1)} all-to-all(bf16[16,32,256]{2,1,0:T(8,128)(2,1)S(1)} %bitcast.13), channel_id=1, replica_groups=mesh['z'=16,'y'=8,'x'=4,'c'=2] {'z'}, dimensions={0} | all-to-all | bytes 524288 | tf_op jit(solution)/shard_map/all_to_all | solution.py:241
  102.2 0.0 copy-done.5
  102.2 0.1 shard_map.82
  102.3 7.4 %all_to_all.32 = bf16[4,32,640]{2,1,0:T(8,128)(2,1)S(1)} all-to-all(bf16[4,32,640]{2,1,0:T(8,128)(2,1)S(1)} %shard_map.82), channel_id=1, replica_groups=mesh['z'=16,'y'=8,'x'=4,'c'=2] {'x'}, dimensions={0} | all-to-all | bytes 327680 | tf_op jit(solution)/shard_map/all_to_all | solution.py:248
  109.7 9.9 %all_gather.3.fact_ref = bf16[256,640]{1,0:T(8,128)(2,1)S(1)} all-gather(bf16[128,640]{1,0:T(8,128)(2,1)S(1)} %bitcast.17), channel_id=1, replica_groups=mesh['z'=16,'y'=8,'x'=4,'c'=2] {'c'}, dimensions={0}, use_global_device_ids=true | all-gather | bytes 491520 | tf_op jit(solution)/shard_map/all_gather | solution.py:176
  119.7 0.0 copy-done.1
  119.7 0.0 copy-done.3
  119.7 1.8 %shard_map.83 = (f32[64,256]{1,0:T(8,128)}, bf16[128,2,256]{2,1,0:T(2,128)(2,1)S(1)}) custom-call(s32[1]{0:T(128)} %bitcast.me_ref, bf16[256,640]{1,0:T(8,128)(2,1)S(1)} %all_gather.3.fact_ref, bf16[256,1024]{1,0:T(8,128)(2,1)S(1)} %copy-done.1, bf16[1024,256]{1,0:T(8,128)(2,1)S(1)} %copy-done.3), custom_call_target="tpu_custom_call" | custom-call | flops 671088640 | bytes 1572868 | tf_op jit(solution)/shard_map/pallas_call | solution.py:47
  121.5 23.7 %all_to_all.33 = bf16[128,2,256]{2,1,0:T(2,128)(2,1)S(1)} all-to-all(bf16[128,2,256]{2,1,0:T(2,128)(2,1)S(1)} %get-tuple-element.21), channel_id=1, replica_groups=mesh['z'=16,'y'=8,'x'=4,'c'=2] {'z','y'}, dimensions={0} | all-to-all | bytes 262144 | tf_op jit(solution)/shard_map/all_to_all | solution.py:258
  145.1 0.2 convert_reduce_fusion
  145.3 0.6 copy.8
  (1 shorter events, 0.0 us)
Async XLA Ops:
  2.4 19.8 %all-to-all-start.1 = ((bf16[8,128,256]{2,1,0:T(8,128)(2,1)}), bf16[8,128,256]{2,1,0:T(8,128)(2,1)S(1)}, u32[]{:S(2)}, u32[]{:S(2)}) async-start(bf16[8,128,256]{2,1,0:T(8,128)(2,1)} %get-tuple-element.13), calls=%async_computation.1 | async-start | bytes 1048576 | tf_op jit(solution)/shard_map/all_to_all | solution.py:204
  10.1 1.0 copy-start
  11.1 1.0 copy-start.2
  12.2 0.7 copy-start.4
  12.9 0.7 copy-start.6
  13.6 0.7 copy-start.7
  22.2 38.1 %all-to-all-start = ((bf16[16,32,256]{2,1,0:T(8,128)(2,1)}), bf16[16,32,256]{2,1,0:T(8,128)(2,1)S(1)}, u32[]{:S(2)}, u32[]{:S(2)}) async-start(bf16[16,32,256]{2,1,0:T(8,128)(2,1)} %get-tuple-element.12), calls=%async_computation | async-start | bytes 524288 | tf_op jit(solution)/shard_map/all_to_all | solution.py:219
  46.6 13.7 %collective-permute-start = (bf16[1024,256]{1,0:T(8,128)(2,1)S(1)}, bf16[1024,256]{1,0:T(8,128)(2,1)S(1)}, u32[]{:S(2)}, u32[]{:S(2)}) collective-permute-start(bf16[1024,256]{1,0:T(8,128)(2,1)S(1)} %bitcast.10), channel_id=1, source_target_pairs={{0,1},{1,0},{2,3},{3,2},{4,5},{5,4},{6,7},{7,6},{8,9},{9,8},{10,11... | collective-permute-start | bytes 1572872 | tf_op jit(solution)/shard_map/ppermute | solution.py:180
  61.2 8.2 %collective-permute-start.1 = (f32[16,128]{1,0:T(8,128)S(1)}, f32[16,128]{1,0:T(8,128)S(1)}, u32[]{:S(2)}, u32[]{:S(2)}) collective-permute-start(f32[16,128]{1,0:T(8,128)S(1)} %get-tuple-element.14.mine_ref), channel_id=1, source_target_pairs={{0,1},{1,0},{2,3},{3,2},{4,5},{5,4},{6,7},{7,6},{8,9},{9,8},{10,11... | collective-permute-start | bytes 24584 | tf_op jit(solution)/shard_map/ppermute | solution.py:180
  83.0 19.3 %copy-start.5 = (bf16[32,256]{1,0:T(8,128)(2,1)S(1)}, bf16[32,256]{1,0:T(8,128)(2,1)}, u32[]{:S(2)}) copy-start(bf16[32,256]{1,0:T(8,128)(2,1)} %get-tuple-element.16.positive_ref) | copy-start | bytes 49156
  83.0 36.7 %copy-start.1 = (bf16[256,1024]{1,0:T(8,128)(2,1)S(1)}, bf16[256,1024]{1,0:T(8,128)(2,1)}, u32[]{:S(2)}) copy-start(bf16[256,1024]{1,0:T(8,128)(2,1)} %w_one_ref.3) | copy-start | bytes 1572868
  83.0 36.7 %copy-start.3 = (bf16[1024,256]{1,0:T(8,128)(2,1)S(1)}, bf16[1024,256]{1,0:T(8,128)(2,1)}, u32[]{:S(2)}) copy-start(bf16[1024,256]{1,0:T(8,128)(2,1)} %w_two_ref.3) | copy-start | bytes 1572868

commit v3 on v2

--- a/solution.py
+++ b/solution.py
@@ -19,7 +19,7 @@
 META = 128
 FACT = EMB + W + META
 
-inv_temperature = 1.0 / 0.02
+score_exponent = 1.4426950408889634 / 0.02
 epsilon = 1e-06
 f32, bf16 = jnp.float32, jnp.bfloat16
 
@@ -75,7 +75,17 @@
 
 
 def tower_kernel(
-    emb_ref, w_one_ref, w_two_ref, owner_ref, slot_ref, spread_ref, dir_ref, scale_ref, base_ref
+    me_ref,
+    emb_ref,
+    w_one_ref,
+    w_two_ref,
+    owner_ref,
+    slot_ref,
+    spread_ref,
+    dir_ref,
+    scale_ref,
+    base_ref,
+    pick_ref,
 ):
     emb = emb_ref[...]
     pair = lax.broadcasted_iota(jnp.int32, (2, META), 0)
@@ -95,6 +105,11 @@
         spread_ref[peer] = unit
     dir_ref[...] = item_dir
     scale_ref[...] = jnp.broadcast_to(scale, (ITEMS, 128))
+    count = H // (NX * NC)
+    hidden_unit = lax.broadcasted_iota(jnp.int32, (H, count), 0)
+    column = lax.broadcasted_iota(jnp.int32, (H, count), 1)
+    chosen = hidden_unit == column * (NX * NC) + me_ref[0]
+    pick_ref[...] = jnp.where(chosen, 1.0, 0.0).astype(bf16)
 
 
 def score_kernel(items_ref, own_ref, other_ref, powers_ref, sums_ref):
@@ -102,8 +117,8 @@
     for step in range(USERS // SCORE_BLOCK):
         users_ref = own_ref if step < USERS // SCORE_BLOCK // 2 else other_ref
         first = step * SCORE_BLOCK % (USERS // 2)
-        scores = nt(items, users_ref[first : first + SCORE_BLOCK, :]) * inv_temperature
-        powers = jnp.exp(scores)
+        exponents = nt(items, users_ref[first : first + SCORE_BLOCK, :]) * score_exponent
+        powers = jnp.exp2(exponents)
         first = step * SCORE_BLOCK
         powers_ref[:, first : first + SCORE_BLOCK] = powers.astype(bf16)
         sums = jnp.sum(powers, axis=0, keepdims=True)
@@ -147,7 +162,7 @@
         spread_ref[peer, :, EMB + META :] = out_cot
 
 
-def grads_kernel(me_ref, fact_ref, w_one_ref, w_two_ref, table_ref, part_ref):
+def grads_kernel(me_ref, fact_ref, w_one_ref, w_two_ref, pick_ref, table_ref, part_ref):
     me = me_ref[0]
     emb = fact_ref[:, :EMB]
     meta = fact_ref[:, EMB : EMB + META].astype(f32)
@@ -164,10 +179,7 @@
     placing = jnp.where((meta[:, 0:1] == mine) & (meta[:, 1:2] == slots), 1.0, 0.0)
     placing += jnp.where((meta[:, 2:3] == mine) & (meta[:, 3:4] == slots), 1.0, 0.0)
     table_ref[...] = tn(placing.astype(bf16), emb_cot.astype(bf16))
-    count = H // (NX * NC)
-    unit = lax.broadcasted_iota(jnp.int32, (H, count), 0)
-    column = lax.broadcasted_iota(jnp.int32, (H, count), 1)
-    pick = jnp.where(unit == column * (NX * NC) + me, 1.0, 0.0).astype(bf16)
+    pick = pick_ref[...]
     part_ref[:, 0, :] = tn(nn(preact_cot, pick).astype(bf16), emb).astype(bf16)
     part_ref[:, 1, :] = tn(nn(hidden, pick).astype(bf16), cot).astype(bf16)
 
@@ -204,16 +216,20 @@
     users = lax.all_to_all(user_spread, "y", 0, 0)
     users = users.reshape(NY * HALF, W)
     others = trade_pair(users)
-    item_spread, item_dir, item_scale, base = call(
+    item_spread, item_dir, item_scale, base, pick = call(
         tower_kernel,
         (
             shape((NZ, ITEMS, W), bf16),
             shape((ITEMS, W), f32),
             shape((ITEMS, 128), f32),
             shape((ITEMS, EMB + META), bf16),
+            shape((H, H // (NX * NC)), bf16),
         ),
-        (item_emb, w_one, w_two, item_owner.T, item_slot.T),
+        (place, item_emb, w_one, w_two, item_owner.T, item_slot.T),
         4 * ITEMS * EMB * H,
+        grid=(),
+        in_specs=[smem, vmem, vmem, vmem, vmem, vmem],
+        out_specs=(vmem,) * 5,
     )
     count = NZ * ITEMS
     items = lax.all_to_all(item_spread, "z", 0, 0).reshape(count, W)
@@ -249,10 +265,10 @@
     table_grad, part = call(
         grads_kernel,
         (shape((TOUCH, EMB), f32), shape((H // (NX * NC), 2, W), bf16)),
-        (place, facts, w_one, w_two),
+        (place, facts, w_one, w_two, pick),
         2 * GROUP * EMB * H * 5,
         grid=(),
-        in_specs=[smem, vmem, vmem, vmem],
+        in_specs=[smem, vmem, vmem, vmem, vmem],
         out_specs=(vmem, vmem),
     )
     part = lax.all_to_all(part, ("z", "y"), 0, 0, tiled=True)

time: 148 us -> 148 us (level)
  no operation moved by 1% of the time
where the time goes in v3:
time: 148 us; the launch traced here: 146 us
  blocking collectives  72.8 us (49%)
  starting transfers between devices  42.1 us (28%)
  waiting for transfers between devices  18.5 us (12%)
  Pallas kernels  6.78 us (5%)
  local copies, waits for them, and re-layouts  4.75 us (3%)
    all_to_all x1, starting transfers between devices, on_device(): items = lax.all_to_all(item_spread, 'z', 0, 0).reshape(count, W)  24.4 us
    all_to_all x1, blocking collectives, on_device(): part = lax.all_to_all(part, ('z', 'y'), 0, 0, tiled=True)  23.7 us
    all_to_all x1, blocking collectives, on_device(): parts = lax.all_to_all(partial.reshape(NZ, ITEMS, W), 'z', 0, 0)  18.2 us
    all_to_all x1, blocking collectives, on_device(): sums = lax.all_to_all(sums, ('y', 'x'), 0, 0)  13.6 us
    all_to_all x1, waiting for transfers between devices, on_device(): items = lax.all_to_all(item_spread, 'z', 0, 0).reshape(count, W)  11 us
    ppermute x2, starting transfers between devices, trade_pair(): return lax.ppermute(values, 'c', [(0, 1), (1, 0)])  10 us
    all_gather x1, blocking collectives, gather_pair(): return lax.all_gather(values, 'c', axis=0, tiled=True)  9.95 us
    all_to_all x1, starting transfers between devices, on_device(): users = lax.all_to_all(user_spread, 'y', 0, 0)  7.66 us
  transfers between devices with their start and end apart: 4, of which 3 were waited for; matrix products, arithmetic and copies ran while one was open for 0% of the time, Pallas kernels for 1%

profile of v3, /device:TPU:1, one launch (start us, length us, event | category | flops | bytes accessed | tf_op | source)
XLA Modules:
  0.0 145.8 jit_solution(14818981046692776255)
XLA Ops:
  0.6 1.8 %shard_map.78 = (bf16[8,128,256]{2,1,0:T(8,128)(2,1)}, bf16[32,256]{1,0:T(8,128)(2,1)}) custom-call(s32[1]{0:T(128)} %bitcast.me_ref, bf16[256,256]{1,0:T(8,128)(2,1)} %user_hbm.1), custom_call_target="tpu_custom_call" | custom-call | flops 131072 | bytes 671748 | tf_op jit(solution)/shard_map/pallas_call | solution.py:47
  2.4 7.7 %all-to-all-start.1 = ((bf16[8,128,256]{2,1,0:T(8,128)(2,1)}), bf16[8,128,256]{2,1,0:T(8,128)(2,1)S(1)}, u32[]{:S(2)}, u32[]{:S(2)}) async-start(bf16[8,128,256]{2,1,0:T(8,128)(2,1)} %get-tuple-element.14), calls=%async_computation.1 | async-start | bytes 1048576 | tf_op jit(solution)/shard_map/all_to_all | solution.py:216
  10.1 0.0 copy-start
  10.1 1.0 copy-done
  11.1 0.0 copy-start.2
  11.1 1.0 copy-done.2
  12.2 0.0 copy-start.4
  12.2 0.7 copy-done.4
  12.9 0.0 copy-start.6
  12.9 0.7 copy-done.6
  13.6 0.0 copy-start.7
  13.6 0.7 copy-done.7
  14.2 1.3 shard_map.77
  15.6 6.7 %all-to-all-done.1 = bf16[8,128,256]{2,1,0:T(8,128)(2,1)S(1)} async-done(((bf16[8,128,256]{2,1,0:T(8,128)(2,1)}), bf16[8,128,256]{2,1,0:T(8,128)(2,1)S(1)}, u32[]{:S(2)}, u32[]{:S(2)}) %all-to-all-start.1) | async-done | bytes 524320 | tf_op jit(solution)/shard_map/all_to_all | solution.py:216
  22.2 24.4 %all-to-all-start = ((bf16[16,32,256]{2,1,0:T(8,128)(2,1)}), bf16[16,32,256]{2,1,0:T(8,128)(2,1)S(1)}, u32[]{:S(2)}, u32[]{:S(2)}) async-start(bf16[16,32,256]{2,1,0:T(8,128)(2,1)} %get-tuple-element.13), calls=%async_computation | async-start | bytes 524288 | tf_op jit(solution)/shard_map/all_to_all | solution.py:235
  46.6 2.7 %collective-permute-start = (bf16[1024,256]{1,0:T(8,128)(2,1)S(1)}, bf16[1024,256]{1,0:T(8,128)(2,1)S(1)}, u32[]{:S(2)}, u32[]{:S(2)}) collective-permute-start(bf16[1024,256]{1,0:T(8,128)(2,1)S(1)} %bitcast.10), channel_id=1, source_target_pairs={{0,1},{1,0},{2,3},{3,2},{4,5},{5,4},{6,7},{7,6},{8,9},{9,8},{10,11... | collective-permute-start | bytes 1572872 | tf_op jit(solution)/shard_map/ppermute | solution.py:192
  49.3 11.0 %all-to-all-done = bf16[16,32,256]{2,1,0:T(8,128)(2,1)S(1)} async-done(((bf16[16,32,256]{2,1,0:T(8,128)(2,1)}), bf16[16,32,256]{2,1,0:T(8,128)(2,1)S(1)}, u32[]{:S(2)}, u32[]{:S(2)}) %all-to-all-start) | async-done | bytes 262176 | tf_op jit(solution)/shard_map/all_to_all | solution.py:235
  60.4 0.0 collective-permute-done.other_ref
  60.4 0.8 shard_map.79
  61.1 7.4 %collective-permute-start.1 = (f32[16,128]{1,0:T(8,128)S(1)}, f32[16,128]{1,0:T(8,128)S(1)}, u32[]{:S(2)}, u32[]{:S(2)}) collective-permute-start(f32[16,128]{1,0:T(8,128)S(1)} %get-tuple-element.15.mine_ref), channel_id=1, source_target_pairs={{0,1},{1,0},{2,3},{3,2},{4,5},{5,4},{6,7},{7,6},{8,9},{9,8},{10,11... | collective-permute-start | bytes 24584 | tf_op jit(solution)/shard_map/ppermute | solution.py:192
  68.5 0.8 collective-permute-done.1.theirs_ref
  69.3 13.6 %all_to_all.30.parts_ref = bf16[32,16,128]{2,1,0:T(8,128)(2,1)S(1)} all-to-all(bf16[32,16,128]{2,1,0:T(8,128)(2,1)S(1)} %shard_map.80), channel_id=1, replica_groups=mesh['z'=16,'y'=8,'x'=4,'c'=2] {'y','x'}, dimensions={0} | all-to-all | bytes 262144 | tf_op jit(solution)/shard_map/all_to_all | solution.py:249
  82.9 0.0 copy-start.5
  82.9 0.0 copy-start.1
  82.9 0.0 copy-start.3
  82.9 1.0 shard_map.81
  83.9 18.2 %all_to_all.31.parts_ref = bf16[16,32,256]{2,1,0:T(8,128)(2,1)S(1)} all-to-all(bf16[16,32,256]{2,1,0:T(8,128)(2,1)S(1)} %bitcast.13), channel_id=1, replica_groups=mesh['z'=16,'y'=8,'x'=4,'c'=2] {'z'}, dimensions={0} | all-to-all | bytes 524288 | tf_op jit(solution)/shard_map/all_to_all | solution.py:257
  102.1 0.0 copy-done.5
  102.1 0.1 shard_map.82
  102.2 7.4 %all_to_all.32 = bf16[4,32,640]{2,1,0:T(8,128)(2,1)S(1)} all-to-all(bf16[4,32,640]{2,1,0:T(8,128)(2,1)S(1)} %shard_map.82), channel_id=1, replica_groups=mesh['z'=16,'y'=8,'x'=4,'c'=2] {'x'}, dimensions={0} | all-to-all | bytes 327680 | tf_op jit(solution)/shard_map/all_to_all | solution.py:264
  109.6 9.9 %all_gather.3.fact_ref = bf16[256,640]{1,0:T(8,128)(2,1)S(1)} all-gather(bf16[128,640]{1,0:T(8,128)(2,1)S(1)} %bitcast.17), channel_id=1, replica_groups=mesh['z'=16,'y'=8,'x'=4,'c'=2] {'c'}, dimensions={0}, use_global_device_ids=true | all-gather | bytes 491520 | tf_op jit(solution)/shard_map/all_gather | solution.py:188
  119.6 0.0 copy-done.1
  119.6 0.0 copy-done.3
  119.6 1.8 %shard_map.83 = (f32[64,256]{1,0:T(8,128)}, bf16[128,2,256]{2,1,0:T(2,128)(2,1)S(1)}) custom-call(s32[1]{0:T(128)} %bitcast.me_ref, bf16[256,640]{1,0:T(8,128)(2,1)S(1)} %all_gather.3.fact_ref, bf16[256,1024]{1,0:T(8,128)(2,1)S(1)} %copy-done.1, bf16[1024,256]{1,0:T(8,128)(2,1)S(1)} %copy-done.3, bf16[1024,128]{1,0:T(8,128)(2,1)S(1)} %get-tuple-element.21.pick_ref), custom_call_target="tpu_custom_call" | custom-call | flops 671088640 | bytes 1835012 | tf_op jit(solution)/shard_map/pallas_call | solution.py:47
  121.4 23.7 %all_to_all.33 = bf16[128,2,256]{2,1,0:T(2,128)(2,1)S(1)} all-to-all(bf16[128,2,256]{2,1,0:T(2,128)(2,1)S(1)} %get-tuple-element.23), channel_id=1, replica_groups=mesh['z'=16,'y'=8,'x'=4,'c'=2] {'z','y'}, dimensions={0} | all-to-all | bytes 262144 | tf_op jit(solution)/shard_map/all_to_all | solution.py:274
  145.1 0.2 convert_reduce_fusion
  145.2 0.6 copy.8
  (1 shorter events, 0.0 us)
Async XLA Ops:
  2.4 19.8 %all-to-all-start.1 = ((bf16[8,128,256]{2,1,0:T(8,128)(2,1)}), bf16[8,128,256]{2,1,0:T(8,128)(2,1)S(1)}, u32[]{:S(2)}, u32[]{:S(2)}) async-start(bf16[8,128,256]{2,1,0:T(8,128)(2,1)} %get-tuple-element.14), calls=%async_computation.1 | async-start | bytes 1048576 | tf_op jit(solution)/shard_map/all_to_all | solution.py:216
  10.1 1.0 copy-start
  11.1 1.0 copy-start.2
  12.2 0.7 copy-start.4
  12.9 0.7 copy-start.6
  13.6 0.7 copy-start.7
  22.2 38.1 %all-to-all-start = ((bf16[16,32,256]{2,1,0:T(8,128)(2,1)}), bf16[16,32,256]{2,1,0:T(8,128)(2,1)S(1)}, u32[]{:S(2)}, u32[]{:S(2)}) async-start(bf16[16,32,256]{2,1,0:T(8,128)(2,1)} %get-tuple-element.13), calls=%async_computation | async-start | bytes 524288 | tf_op jit(solution)/shard_map/all_to_all | solution.py:235
  46.6 13.7 %collective-permute-start = (bf16[1024,256]{1,0:T(8,128)(2,1)S(1)}, bf16[1024,256]{1,0:T(8,128)(2,1)S(1)}, u32[]{:S(2)}, u32[]{:S(2)}) collective-permute-start(bf16[1024,256]{1,0:T(8,128)(2,1)S(1)} %bitcast.10), channel_id=1, source_target_pairs={{0,1},{1,0},{2,3},{3,2},{4,5},{5,4},{6,7},{7,6},{8,9},{9,8},{10,11... | collective-permute-start | bytes 1572872 | tf_op jit(solution)/shard_map/ppermute | solution.py:192
  61.1 8.2 %collective-permute-start.1 = (f32[16,128]{1,0:T(8,128)S(1)}, f32[16,128]{1,0:T(8,128)S(1)}, u32[]{:S(2)}, u32[]{:S(2)}) collective-permute-start(f32[16,128]{1,0:T(8,128)S(1)} %get-tuple-element.15.mine_ref), channel_id=1, source_target_pairs={{0,1},{1,0},{2,3},{3,2},{4,5},{5,4},{6,7},{7,6},{8,9},{9,8},{10,11... | collective-permute-start | bytes 24584 | tf_op jit(solution)/shard_map/ppermute | solution.py:192
  82.9 19.3 %copy-start.5 = (bf16[32,256]{1,0:T(8,128)(2,1)S(1)}, bf16[32,256]{1,0:T(8,128)(2,1)}, u32[]{:S(2)}) copy-start(bf16[32,256]{1,0:T(8,128)(2,1)} %get-tuple-element.17.positive_ref) | copy-start | bytes 49156
  82.9 36.7 %copy-start.1 = (bf16[256,1024]{1,0:T(8,128)(2,1)S(1)}, bf16[256,1024]{1,0:T(8,128)(2,1)}, u32[]{:S(2)}) copy-start(bf16[256,1024]{1,0:T(8,128)(2,1)} %w_one_ref.3) | copy-start | bytes 1572868
  82.9 36.7 %copy-start.3 = (bf16[1024,256]{1,0:T(8,128)(2,1)S(1)}, bf16[1024,256]{1,0:T(8,128)(2,1)}, u32[]{:S(2)}) copy-start(bf16[1024,256]{1,0:T(8,128)(2,1)} %w_two_ref.3) | copy-start | bytes 1572868

commit v4 on v3

--- a/solution.py
+++ b/solution.py
@@ -134,18 +134,22 @@
     spread_ref[...] = jnp.broadcast_to(total.astype(bf16)[None], spread_ref.shape)
 
 
-def unit_cot_kernel(parts_ref, own_ref, other_ref, powers_ref, out_ref, scaled_ref):
+def unit_cot_kernel(parts_ref, own_ref, other_ref, powers_ref, out_ref):
     half = USERS // 128 // 2
     totals = parts_ref[0].astype(f32)
     for peer in range(1, NY * NX):
         totals += parts_ref[peer].astype(f32)
     inverse = jnp.transpose(1.0 / totals)
-    for k in range(USERS // 128):
-        users_ref = own_ref if k < half else other_ref
-        first = k % half * 128
-        block = users_ref[first : first + 128, :].astype(f32) * inverse[:, k : k + 1]
-        scaled_ref[k * 128 : (k + 1) * 128, :] = block.astype(bf16)
-    out_ref[...] = nn(powers_ref[...], scaled_ref[...]).astype(bf16)
+    total = None
+    for first in range(0, USERS, 512):
+        scaled = []
+        for k in range(first // 128, first // 128 + 4):
+            users_ref = own_ref if k < half else other_ref
+            rows = slice(k % half * 128, k % half * 128 + 128)
+            scaled.append((users_ref[rows, :].astype(f32) * inverse[:, k : k + 1]).astype(bf16))
+        product = nn(powers_ref[:, first : first + 512], jnp.concatenate(scaled, axis=0))
+        total = product if total is None else total + product
+    out_ref[...] = total.astype(bf16)
 
 
 def cot_kernel(parts_ref, positive_ref, dir_ref, scale_ref, base_ref, spread_ref):
@@ -252,7 +256,6 @@
         (shape((count, W), bf16),),
         (sums, users, others, powers),
         2 * count * USERS * W,
-        scratch=(pltpu.VMEM((USERS, W), bf16),),
     )[0]
     parts = lax.all_to_all(partial.reshape(NZ, ITEMS, W), "z", 0, 0)
     facts = call(

time: 148 us -> 148 us (level)
  no operation moved by 1% of the time
where the time goes in v4:
time: 148 us; the launch traced here: 146 us
  blocking collectives  72.8 us (49%)
  starting transfers between devices  42.1 us (28%)
  waiting for transfers between devices  18.5 us (12%)
  Pallas kernels  6.78 us (5%)
  local copies, waits for them, and re-layouts  4.75 us (3%)
    all_to_all x1, starting transfers between devices, on_device(): items = lax.all_to_all(item_spread, 'z', 0, 0).reshape(count, W)  24.4 us
    all_to_all x1, blocking collectives, on_device(): part = lax.all_to_all(part, ('z', 'y'), 0, 0, tiled=True)  23.7 us
    all_to_all x1, blocking collectives, on_device(): parts = lax.all_to_all(partial.reshape(NZ, ITEMS, W), 'z', 0, 0)  18.2 us
    all_to_all x1, blocking collectives, on_device(): sums = lax.all_to_all(sums, ('y', 'x'), 0, 0)  13.6 us
    all_to_all x1, waiting for transfers between devices, on_device(): items = lax.all_to_all(item_spread, 'z', 0, 0).reshape(count, W)  11 us
    ppermute x2, starting transfers between devices, trade_pair(): return lax.ppermute(values, 'c', [(0, 1), (1, 0)])  10 us
    all_gather x1, blocking collectives, gather_pair(): return lax.all_gather(values, 'c', axis=0, tiled=True)  9.96 us
    all_to_all x1, starting transfers between devices, on_device(): users = lax.all_to_all(user_spread, 'y', 0, 0)  7.66 us
  transfers between devices with their start and end apart: 4, of which 3 were waited for; matrix products, arithmetic and copies ran while one was open for 0% of the time, Pallas kernels for 1%

profile of v4, /device:TPU:1, one launch (start us, length us, event | category | flops | bytes accessed | tf_op | source)
XLA Modules:
  0.0 145.8 jit_solution(15676915894632869332)
XLA Ops:
  0.6 1.8 %shard_map.78 = (bf16[8,128,256]{2,1,0:T(8,128)(2,1)}, bf16[32,256]{1,0:T(8,128)(2,1)}) custom-call(s32[1]{0:T(128)} %bitcast.me_ref, bf16[256,256]{1,0:T(8,128)(2,1)} %user_hbm.1), custom_call_target="tpu_custom_call" | custom-call | flops 131072 | bytes 671748 | tf_op jit(solution)/shard_map/pallas_call | solution.py:47
  2.4 7.7 %all-to-all-start.1 = ((bf16[8,128,256]{2,1,0:T(8,128)(2,1)}), bf16[8,128,256]{2,1,0:T(8,128)(2,1)S(1)}, u32[]{:S(2)}, u32[]{:S(2)}) async-start(bf16[8,128,256]{2,1,0:T(8,128)(2,1)} %get-tuple-element.14), calls=%async_computation.1 | async-start | bytes 1048576 | tf_op jit(solution)/shard_map/all_to_all | solution.py:220
  10.1 0.0 copy-start
  10.1 1.0 copy-done
  11.1 0.0 copy-start.2
  11.1 1.0 copy-done.2
  12.2 0.0 copy-start.4
  12.2 0.7 copy-done.4
  12.9 0.0 copy-start.6
  12.9 0.7 copy-done.6
  13.6 0.0 copy-start.7
  13.6 0.7 copy-done.7
  14.2 1.3 shard_map.77
  15.6 6.7 %all-to-all-done.1 = bf16[8,128,256]{2,1,0:T(8,128)(2,1)S(1)} async-done(((bf16[8,128,256]{2,1,0:T(8,128)(2,1)}), bf16[8,128,256]{2,1,0:T(8,128)(2,1)S(1)}, u32[]{:S(2)}, u32[]{:S(2)}) %all-to-all-start.1) | async-done | bytes 524320 | tf_op jit(solution)/shard_map/all_to_all | solution.py:220
  22.2 24.4 %all-to-all-start = ((bf16[16,32,256]{2,1,0:T(8,128)(2,1)}), bf16[16,32,256]{2,1,0:T(8,128)(2,1)S(1)}, u32[]{:S(2)}, u32[]{:S(2)}) async-start(bf16[16,32,256]{2,1,0:T(8,128)(2,1)} %get-tuple-element.13), calls=%async_computation | async-start | bytes 524288 | tf_op jit(solution)/shard_map/all_to_all | solution.py:239
  46.6 2.7 %collective-permute-start = (bf16[1024,256]{1,0:T(8,128)(2,1)S(1)}, bf16[1024,256]{1,0:T(8,128)(2,1)S(1)}, u32[]{:S(2)}, u32[]{:S(2)}) collective-permute-start(bf16[1024,256]{1,0:T(8,128)(2,1)S(1)} %bitcast.10), channel_id=1, source_target_pairs={{0,1},{1,0},{2,3},{3,2},{4,5},{5,4},{6,7},{7,6},{8,9},{9,8},{10,11... | collective-permute-start | bytes 1572872 | tf_op jit(solution)/shard_map/ppermute | solution.py:196
  49.3 11.0 %all-to-all-done = bf16[16,32,256]{2,1,0:T(8,128)(2,1)S(1)} async-done(((bf16[16,32,256]{2,1,0:T(8,128)(2,1)}), bf16[16,32,256]{2,1,0:T(8,128)(2,1)S(1)}, u32[]{:S(2)}, u32[]{:S(2)}) %all-to-all-start) | async-done | bytes 262176 | tf_op jit(solution)/shard_map/all_to_all | solution.py:239
  60.4 0.0 collective-permute-done.other_ref
  60.4 0.8 shard_map.79
  61.1 7.4 %collective-permute-start.1 = (f32[16,128]{1,0:T(8,128)S(1)}, f32[16,128]{1,0:T(8,128)S(1)}, u32[]{:S(2)}, u32[]{:S(2)}) collective-permute-start(f32[16,128]{1,0:T(8,128)S(1)} %get-tuple-element.15.mine_ref), channel_id=1, source_target_pairs={{0,1},{1,0},{2,3},{3,2},{4,5},{5,4},{6,7},{7,6},{8,9},{9,8},{10,11... | collective-permute-start | bytes 24584 | tf_op jit(solution)/shard_map/ppermute | solution.py:196
  68.5 0.8 collective-permute-done.1.theirs_ref
  69.3 13.6 %all_to_all.30.parts_ref = bf16[32,16,128]{2,1,0:T(8,128)(2,1)S(1)} all-to-all(bf16[32,16,128]{2,1,0:T(8,128)(2,1)S(1)} %shard_map.80), channel_id=1, replica_groups=mesh['z'=16,'y'=8,'x'=4,'c'=2] {'y','x'}, dimensions={0} | all-to-all | bytes 262144 | tf_op jit(solution)/shard_map/all_to_all | solution.py:253
  82.9 0.0 copy-start.5
  82.9 0.0 copy-start.1
  82.9 0.0 copy-start.3
  82.9 1.0 shard_map.81
  83.9 18.2 %all_to_all.31.parts_ref = bf16[16,32,256]{2,1,0:T(8,128)(2,1)S(1)} all-to-all(bf16[16,32,256]{2,1,0:T(8,128)(2,1)S(1)} %bitcast.13), channel_id=1, replica_groups=mesh['z'=16,'y'=8,'x'=4,'c'=2] {'z'}, dimensions={0} | all-to-all | bytes 524288 | tf_op jit(solution)/shard_map/all_to_all | solution.py:260
  102.1 0.0 copy-done.5
  102.1 0.1 shard_map.82
  102.2 7.4 %all_to_all.32 = bf16[4,32,640]{2,1,0:T(8,128)(2,1)S(1)} all-to-all(bf16[4,32,640]{2,1,0:T(8,128)(2,1)S(1)} %shard_map.82), channel_id=1, replica_groups=mesh['z'=16,'y'=8,'x'=4,'c'=2] {'x'}, dimensions={0} | all-to-all | bytes 327680 | tf_op jit(solution)/shard_map/all_to_all | solution.py:267
  109.6 10.0 %all_gather.3.fact_ref = bf16[256,640]{1,0:T(8,128)(2,1)S(1)} all-gather(bf16[128,640]{1,0:T(8,128)(2,1)S(1)} %bitcast.17), channel_id=1, replica_groups=mesh['z'=16,'y'=8,'x'=4,'c'=2] {'c'}, dimensions={0}, use_global_device_ids=true | all-gather | bytes 491520 | tf_op jit(solution)/shard_map/all_gather | solution.py:192
  119.6 0.0 copy-done.1
  119.6 0.0 copy-done.3
  119.6 1.8 %shard_map.83 = (f32[64,256]{1,0:T(8,128)}, bf16[128,2,256]{2,1,0:T(2,128)(2,1)S(1)}) custom-call(s32[1]{0:T(128)} %bitcast.me_ref, bf16[256,640]{1,0:T(8,128)(2,1)S(1)} %all_gather.3.fact_ref, bf16[256,1024]{1,0:T(8,128)(2,1)S(1)} %copy-done.1, bf16[1024,256]{1,0:T(8,128)(2,1)S(1)} %copy-done.3, bf16[1024,128]{1,0:T(8,128)(2,1)S(1)} %get-tuple-element.21.pick_ref), custom_call_target="tpu_custom_call" | custom-call | flops 671088640 | bytes 1835012 | tf_op jit(solution)/shard_map/pallas_call | solution.py:47
  121.4 23.7 %all_to_all.33 = bf16[128,2,256]{2,1,0:T(2,128)(2,1)S(1)} all-to-all(bf16[128,2,256]{2,1,0:T(2,128)(2,1)S(1)} %get-tuple-element.23), channel_id=1, replica_groups=mesh['z'=16,'y'=8,'x'=4,'c'=2] {'z','y'}, dimensions={0} | all-to-all | bytes 262144 | tf_op jit(solution)/shard_map/all_to_all | solution.py:277
  145.0 0.2 convert_reduce_fusion
  145.2 0.6 copy.8
  (1 shorter events, 0.0 us)
Async XLA Ops:
  2.4 19.8 %all-to-all-start.1 = ((bf16[8,128,256]{2,1,0:T(8,128)(2,1)}), bf16[8,128,256]{2,1,0:T(8,128)(2,1)S(1)}, u32[]{:S(2)}, u32[]{:S(2)}) async-start(bf16[8,128,256]{2,1,0:T(8,128)(2,1)} %get-tuple-element.14), calls=%async_computation.1 | async-start | bytes 1048576 | tf_op jit(solution)/shard_map/all_to_all | solution.py:220
  10.1 1.0 copy-start
  11.1 1.0 copy-start.2
  12.2 0.7 copy-start.4
  12.9 0.7 copy-start.6
  13.6 0.7 copy-start.7
  22.2 38.1 %all-to-all-start = ((bf16[16,32,256]{2,1,0:T(8,128)(2,1)}), bf16[16,32,256]{2,1,0:T(8,128)(2,1)S(1)}, u32[]{:S(2)}, u32[]{:S(2)}) async-start(bf16[16,32,256]{2,1,0:T(8,128)(2,1)} %get-tuple-element.13), calls=%async_computation | async-start | bytes 524288 | tf_op jit(solution)/shard_map/all_to_all | solution.py:239
  46.6 13.7 %collective-permute-start = (bf16[1024,256]{1,0:T(8,128)(2,1)S(1)}, bf16[1024,256]{1,0:T(8,128)(2,1)S(1)}, u32[]{:S(2)}, u32[]{:S(2)}) collective-permute-start(bf16[1024,256]{1,0:T(8,128)(2,1)S(1)} %bitcast.10), channel_id=1, source_target_pairs={{0,1},{1,0},{2,3},{3,2},{4,5},{5,4},{6,7},{7,6},{8,9},{9,8},{10,11... | collective-permute-start | bytes 1572872 | tf_op jit(solution)/shard_map/ppermute | solution.py:196
  61.1 8.2 %collective-permute-start.1 = (f32[16,128]{1,0:T(8,128)S(1)}, f32[16,128]{1,0:T(8,128)S(1)}, u32[]{:S(2)}, u32[]{:S(2)}) collective-permute-start(f32[16,128]{1,0:T(8,128)S(1)} %get-tuple-element.15.mine_ref), channel_id=1, source_target_pairs={{0,1},{1,0},{2,3},{3,2},{4,5},{5,4},{6,7},{7,6},{8,9},{9,8},{10,11... | collective-permute-start | bytes 24584 | tf_op jit(solution)/shard_map/ppermute | solution.py:196
  82.9 19.3 %copy-start.5 = (bf16[32,256]{1,0:T(8,128)(2,1)S(1)}, bf16[32,256]{1,0:T(8,128)(2,1)}, u32[]{:S(2)}) copy-start(bf16[32,256]{1,0:T(8,128)(2,1)} %get-tuple-element.17.positive_ref) | copy-start | bytes 49156
  82.9 36.7 %copy-start.1 = (bf16[256,1024]{1,0:T(8,128)(2,1)S(1)}, bf16[256,1024]{1,0:T(8,128)(2,1)}, u32[]{:S(2)}) copy-start(bf16[256,1024]{1,0:T(8,128)(2,1)} %w_one_ref.3) | copy-start | bytes 1572868
  82.9 36.7 %copy-start.3 = (bf16[1024,256]{1,0:T(8,128)(2,1)S(1)}, bf16[1024,256]{1,0:T(8,128)(2,1)}, u32[]{:S(2)}) copy-start(bf16[1024,256]{1,0:T(8,128)(2,1)} %w_two_ref.3) | copy-start | bytes 1572868
